TPU v7x, 32 devices: a whole 2x2x4 slice. The times are simulated.
32 devices in a mesh: dp: 8 (over y, x, core), ctx: 4 (over z).
Axes of the slice: x: 2, y: 2, z: 4, core: 2. Of those that a mesh axis runs over, the one named last changes fastest.
Arguments:
- queries: bfloat16 [32768, 8, 128], P(('dp', 'ctx')), parts along dimension 0, may hold values from -6 to 6
- keys: bfloat16 [32768, 128], P(('dp', 'ctx')), parts along dimension 0, may hold values from -6 to 6
- values: bfloat16 [32768, 128], P(('dp', 'ctx')), parts along dimension 0, may hold values from -6 to 6
- output: bfloat16 [32768, 8, 128], P(('dp', 'ctx')), parts along dimension 0, may hold values from -6 to 6
- d_output: bfloat16 [32768, 8, 128], P(('dp', 'ctx')), parts along dimension 0, may hold values from -6 to 6
- block_lists: int32 [128, 3], P('dp'), parts along dimension 0, may hold values from -1 to 15, as said below
Outputs:
- d_queries: bfloat16 [32768, 8, 128], P(('dp', 'ctx')), parts along dimension 0
- d_keys: bfloat16 [32768, 128], P(('dp', 'ctx')), parts along dimension 0
- d_values: bfloat16 [32768, 128], P(('dp', 'ctx')), parts along dimension 0
There are 8 independent parts, one for each index of `dp`. A program takes and returns all parts, laid end to end along the dimension named above; each array names one. Nothing has to cross between parts.
Inputs may be any that keep to these rules, and one draw needn't show every extreme that they name: `block_lists`: row b: entry 0 is b itself; the other 2 entries are distinct blocks below b, or -1 where fewer than 2 blocks lie below b.
All inputs are finite; a program needn't handle non-finite values.
Results may differ from a plain program's by a relative error of at most 0.005.
Values may be sent and summed in bfloat16 or wider, within the bound.
A program may use at most 192 MiB of HBM per device.

v0:
```python
import jax
import jax.numpy as jnp
from jax import lax
from jax.sharding import PartitionSpec as P

BLK = 256
TOPK = 3


def shards(queries, keys, values, output, d_output, block_lists):
    shard_rows = queries.shape[0]
    head_dim = queries.shape[2]
    group_size = lax.axis_size("ctx")
    my_index = lax.axis_index("ctx")
    scaling = head_dim ** (-0.5)
    paired = jnp.concatenate([keys, values], axis=1)
    everything = lax.all_gather(paired, "ctx", axis=0, tiled=True)
    grad_terms = jnp.zeros((group_size * shard_rows, 2 * head_dim), jnp.float32)
    local_count = shard_rows // BLK
    query_grads = []
    for local_block in range(local_count):
        global_block = my_index * local_count + local_block
        chosen = lax.dynamic_index_in_dim(block_lists, global_block, 0, keepdims=False)
        q_block = queries[local_block * BLK : (local_block + 1) * BLK]
        o_block = output[local_block * BLK : (local_block + 1) * BLK]
        g_block = d_output[local_block * BLK : (local_block + 1) * BLK]
        query_pos = global_block * BLK + jnp.arange(BLK, dtype=jnp.int32)
        starts = []
        pieces = []
        masked = []
        for slot_index in range(TOPK):
            wanted = chosen[slot_index]
            start_row = jnp.maximum(wanted, 0) * BLK
            kv_block = lax.dynamic_slice_in_dim(everything, start_row, BLK, 0)
            raw = (
                jnp.einsum(
                    "qhd,kd->hqk",
                    q_block,
                    kv_block[:, :head_dim],
                    preferred_element_type=jnp.float32,
                )
                * scaling
            )
            key_pos = start_row + jnp.arange(BLK, dtype=jnp.int32)
            allowed = (wanted >= 0) & (key_pos[None, :] <= query_pos[:, None])
            starts.append(start_row)
            pieces.append(kv_block)
            masked.append(jnp.where(allowed[None], raw, -jnp.inf))
        top = masked[0].max(axis=2)
        for slot_index in range(1, TOPK):
            top = jnp.maximum(top, masked[slot_index].max(axis=2))
        exps = [jnp.exp(entry - top[:, :, None]) for entry in masked]
        total = exps[0].sum(axis=2)
        for slot_index in range(1, TOPK):
            total = total + exps[slot_index].sum(axis=2)
        delta = jnp.transpose(
            jnp.sum(g_block.astype(jnp.float32) * o_block.astype(jnp.float32), axis=2)
        )
        query_acc = jnp.zeros((BLK, queries.shape[1], head_dim), jnp.float32)
        for slot_index in range(TOPK):
            kv_block = pieces[slot_index]
            key_block = kv_block[:, :head_dim]
            prob = exps[slot_index] / total[:, :, None]
            d_prob = jnp.einsum(
                "qhd,kd->hqk", g_block, kv_block[:, head_dim:], preferred_element_type=jnp.float32
            )
            d_scores = (prob * (d_prob - delta[:, :, None])).astype(jnp.bfloat16)
            value_part = jnp.einsum(
                "hqk,qhd->kd",
                prob.astype(jnp.bfloat16),
                g_block,
                preferred_element_type=jnp.float32,
            )
            key_part = (
                jnp.einsum("hqk,qhd->kd", d_scores, q_block, preferred_element_type=jnp.float32)
                * scaling
            )
            query_acc = query_acc + jnp.einsum(
                "hqk,kd->qhd", d_scores, key_block, preferred_element_type=jnp.float32
            )
            existing = lax.dynamic_slice_in_dim(grad_terms, starts[slot_index], BLK, 0)
            grad_terms = lax.dynamic_update_slice_in_dim(
                grad_terms,
                existing + jnp.concatenate([key_part, value_part], axis=1),
                starts[slot_index],
                0,
            )
        query_grads.append((query_acc * scaling).astype(jnp.bfloat16))
    d_queries = jnp.concatenate(query_grads, axis=0)
    mine = lax.psum_scatter(grad_terms, "ctx", scatter_dimension=0, tiled=True)
    return (
        d_queries,
        mine[:, :head_dim].astype(jnp.bfloat16),
        mine[:, head_dim:].astype(jnp.bfloat16),
    )


def solution(mesh):
    return jax.shard_map(
        shards,
        mesh=mesh,
        in_specs=(
            P(("dp", "ctx"), None, None),
            P(("dp", "ctx"), None),
            P(("dp", "ctx"), None),
            P(("dp", "ctx"), None, None),
            P(("dp", "ctx"), None, None),
            P("dp", None),
        ),
        out_specs=(P(("dp", "ctx"), None, None), P(("dp", "ctx"), None), P(("dp", "ctx"), None)),
        check_vma=False,
    )
```

profile of v0, /device:TPU:0, one launch (start us, length us, event | category | flops | bytes accessed | tf_op | source)
XLA Modules:
  0.0 203.2 jit_solution(7434673309509727322)
XLA Ops:
  7.2 2.0 pad_maximum_fusion.1
  28.7 1.5 copy-done.21
  31.1 1.3 multiply_reduce_fusion.2
  33.4 25.5 %all-gather.2.cloned.1.call-done = bf16[4096,256]{1,0:T(8,128)(2,1)} async-done(((bf16[1024,256]{1,0:T(8,128)(2,1)}), bf16[4096,256]{1,0:T(8,128)(2,1)}) %all-gather.2.cloned.1.call-update) | async-done | bytes 2097168 | tf_op jit(solution)/shard_map/all_gather | solution.py:17
  58.8 1.5 fusion.200
  95.3 2.4 %broadcast_in_dim.166 = f32[4096,256]{0,1:T(8,128)} broadcast(f32[]{:T(128)} %constant.76.clone.1), dimensions={} | broadcast | bytes 4194308 | tf_op jit(solution)/shard_map/broadcast_in_dim | solution.py:18
  98.5 1.7 fusion.96
  100.2 1.7 fusion.97
  102.0 1.7 fusion.98
  103.7 1.7 fusion.99
  105.4 1.7 fusion.100
  107.1 1.7 fusion.101
  108.9 1.7 fusion.102
  110.6 1.7 fusion.103
  112.3 1.7 fusion.104
  114.1 1.7 fusion.105
  115.8 1.7 fusion.106
  122.6 1.3 convolution_add_fusion.7
  126.6 1.3 fusion.58
  127.9 1.3 convolution_add_fusion.3
  129.2 1.3 fusion.57
  133.2 2.9 %copy.93 = bf16[1024,8,128]{2,1,0:T(8,128)(2,1)} copy(bf16[1024,8,128]{0,2,1:T(8,128)(2,1)S(1)} %pad_maximum_fusion) | data formatting | bytes 4194304
  136.1 57.1 %reduce-scatter.2.cloned.1.call-done = f32[1024,256]{0,1:T(8,128)} async-done(((f32[4096,256]{0,1:T(8,128)}), f32[1024,256]{0,1:T(8,128)}) %reduce-scatter.2.cloned.1.call-update) | async-done | bytes 1048592 | tf_op jit(solution)/shard_map/reduce_scatter | solution.py:90
  193.3 1.3 convert.4
  (180 shorter events, 53.5 us)
Async XLA Ops:
  7.2 21.3 %copy-start.20 = (bf16[1024,8,128]{2,1,0:T(8,128)(2,1)S(1)}, bf16[1024,8,128]{2,1,0:T(8,128)(2,1)}, u32[]{:S(2)}) copy-start(bf16[1024,8,128]{2,1,0:T(8,128)(2,1)} %param.10) | copy-start | bytes 6291460
  7.2 51.7 %all-gather.2.cloned.1.call-start = ((), (), s32[]{:S(2)}) async-start(), calls=%async_computation.1 | async-start | bytes 2621440 | tf_op jit(solution)/shard_map/all_gather | solution.py:17
  9.3 184.0 %reduce-scatter.2.cloned.1.call-start = ((), (), s32[]{:S(2)}) async-start(), calls=%async_computation.2 | async-start | bytes 5242880 | tf_op jit(solution)/shard_map/reduce_scatter | solution.py:90
  28.5 1.6 copy-start.21
  30.1 42.5 %copy-start.25 = (bf16[256,8,128]{2,1,0:T(8,128)(2,1)}, bf16[256,8,128]{2,1,0:T(8,128)(2,1)S(1)}, u32[]{:S(2)}) copy-start(bf16[256,8,128]{2,1,0:T(8,128)(2,1)S(1)} %get-tuple-element.23) | copy-start | bytes 1572868
  30.1 46.7 %copy-start.23 = (bf16[256,8,128]{2,1,0:T(8,128)(2,1)}, bf16[256,8,128]{2,1,0:T(8,128)(2,1)S(1)}, u32[]{:S(2)}) copy-start(bf16[256,8,128]{2,1,0:T(8,128)(2,1)S(1)} %get-tuple-element.25) | copy-start | bytes 1572868
  31.1 2.1 %copy-start.22 = (bf16[1024,8,128]{2,1,0:T(8,128)(2,1)S(1)}, bf16[1024,8,128]{2,1,0:T(8,128)(2,1)}, u32[]{:S(2)}) copy-start(bf16[1024,8,128]{2,1,0:T(8,128)(2,1)} %param.6) | copy-start | bytes 6291460
  58.8 1.7 copy-start.31
  58.8 1.7 copy-start.36
  58.8 2.1 %copy-start.35 = (pred[256,256]{0,1:T(8,128)(4,1)S(1)}, pred[256,256]{0,1:T(8,128)(4,1)}, u32[]{:S(2)}) copy-start(pred[256,256]{0,1:T(8,128)(4,1)} %get-tuple-element.49) | copy-start | bytes 196612
  81.4 1.1 copy-start.4
  85.9 1.3 copy-start.8
  90.4 1.1 copy-start.12
  94.8 2.9 %copy-start.16 = (bf16[8,256,256]{1,2,0:T(8,128)(2,1)}, bf16[8,256,256]{1,2,0:T(8,128)(2,1)S(1)}, u32[]{:S(2)}) copy-start(bf16[8,256,256]{1,2,0:T(8,128)(2,1)S(1)} %fusion.1) | copy-start | bytes 3145732
  117.5 1.3 copy-start.1
  118.8 2.6 %copy-start.3 = (bf16[8,256,256]{1,2,0:T(8,128)(2,1)S(1)}, bf16[8,256,256]{1,2,0:T(8,128)(2,1)}, u32[]{:S(2)}) copy-start(bf16[8,256,256]{1,2,0:T(8,128)(2,1)} %copy-done.2) | copy-start | bytes 3145732
  120.1 2.5 %copy-start.7 = (bf16[8,256,256]{1,2,0:T(8,128)(2,1)S(1)}, bf16[8,256,256]{1,2,0:T(8,128)(2,1)}, u32[]{:S(2)}) copy-start(bf16[8,256,256]{1,2,0:T(8,128)(2,1)} %copy-done.6) | copy-start | bytes 3145732
  122.6 1.5 copy-start.5
  124.1 1.3 copy-start.11
  125.3 1.3 copy-start.9
  126.6 1.3 copy-start.15
  127.9 1.3 copy-start.13
  129.2 1.3 copy-start.19
  130.5 1.3 copy-start.17
  (17 other events, 17.0 us)
Sparse Core Ops, SparseCore 0:
  10.2 48.6 all-gather.1
  117.7 75.5 reduce-scatter.1
where the time goes:
time: 204 us; the launch traced here: 203 us
  waiting for transfers between devices  82.6 us (40%)
  matrix products  42.1 us (21%)
  other arithmetic  31.5 us (15%)
  between operations  30 us (15%)
  local copies, waits for them, and re-layouts  16.8 us (8%)
    reduce_scatter x1, waiting for transfers between devices, shards(): mine = lax.psum_scatter(grad_terms, 'ctx', scatter_dimension=0, tiled=True)  57.1 us
    all_gather x1, waiting for transfers between devices, shards(): everything = lax.all_gather(paired, 'ctx', axis=0, tiled=True)  25.5 us
    dynamic_update_slice x12, other arithmetic, shards(): lax.dynamic_update_slice_in_dim(grad_terms, existing + jnp.concatenate([k...  19.7 us
    dot_general x12, matrix products, shards(): jnp.einsum('hqk,kd->qhd', d_scores, key_block, preferred_element_type=jnp...  15 us
    unnamed x81, local copies, waits for them, and re-layouts  11.9 us
    dot_general x12, matrix products, shards(): jnp.einsum('qhd,kd->hqk', g_block, kv_block[:, head_dim:], preferred_elem...  7.51 us
    dot_general x12, matrix products, shards(): jnp.einsum('hqk,qhd->kd', prob.astype(jnp.bfloat16), g_block, preferred_e...  6.89 us
    dot_general x12, matrix products, shards(): jnp.einsum('qhd,kd->hqk', q_block, kv_block[:, :head_dim], preferred_elem...  6.84 us
  transfers between devices with their start and end apart: 2, of which 2 were waited for; matrix products, arithmetic and copies ran while one was open for 12% of the time, Pallas kernels for 0%

commit v1 on v0

v1 whole, which is shorter than its diff:
```python
import functools

import jax
import jax.numpy as jnp
from jax import lax
from jax.experimental import pallas as pl
from jax.experimental.pallas import tpu as pltpu
from jax.sharding import PartitionSpec as P

BLK = 256
TOPK = 3
CH = 256
MESH = pl.DeviceIdType.MESH
LOG2E = 1.4426950408889634


def kernel(
    n, nb, heads, hd,
    lists, q_hbm, k_hbm, v_hbm, o_hbm, g_hbm,
    dq_hbm, dk_hbm, dv_hbm,
    q, g, o, qt, gt, delta, probs, kfull, vfull, kcat, kcat_t, vcat,
    part_v, part_k, dvbuf, dkbuf,
    in_sem, out_sem, own_sem,
    k_send, k_recv, v_send, v_recv, dv_send, dv_recv, dk_send, dk_recv,
):
    me = lax.axis_index("ctx")
    rows = BLK * heads
    nch = rows // CH
    scaling = hd ** (-0.5)
    last = n - 1

    def up(hbm, full, send, recv, owner, own):
        src = hbm if own else full.at[pl.ds(owner * nb, nb)]
        return pltpu.make_async_remote_copy(
            src_ref=src,
            dst_ref=full.at[pl.ds(owner * nb, nb)],
            send_sem=send.at[owner],
            recv_sem=recv.at[owner],
            device_id={"ctx": me + 1},
            device_id_type=MESH,
        )

    k_up = functools.partial(up, k_hbm, kfull, k_send, k_recv)
    v_up = functools.partial(up, v_hbm, vfull, v_send, v_recv)

    def down(buf, send, recv, owner):
        return pltpu.make_async_remote_copy(
            src_ref=buf.at[owner],
            dst_ref=buf.at[owner],
            send_sem=send.at[owner],
            recv_sem=recv.at[owner],
            device_id={"ctx": me - 1},
            device_id_type=MESH,
        )

    dv_down = functools.partial(down, dvbuf, dv_send, dv_recv)
    dk_down = functools.partial(down, dkbuf, dk_send, dk_recv)

    def in_copy(lb, which):
        src, dst = ((q_hbm, q), (g_hbm, g), (o_hbm, o))[which]
        return pltpu.make_async_copy(src.at[lb], dst.at[lb], in_sem.at[which, lb])

    def dq_copy(lb):
        return pltpu.make_async_copy(o.at[lb], dq_hbm.at[lb], out_sem.at[lb])

    own_k = pltpu.make_async_copy(k_hbm, kfull.at[pl.ds(me * nb, nb)], own_sem.at[0])
    own_v = pltpu.make_async_copy(v_hbm, vfull.at[pl.ds(me * nb, nb)], own_sem.at[1])

    barrier = pltpu.get_barrier_semaphore()

    @pl.when(me > 0)
    def _():
        pl.semaphore_signal(barrier, inc=1, device_id={"ctx": me - 1}, device_id_type=MESH)

    @pl.when(me < last)
    def _():
        pl.semaphore_signal(barrier, inc=1, device_id={"ctx": me + 1}, device_id_type=MESH)

    pl.semaphore_wait(barrier, jnp.where(me > 0, 1, 0) + jnp.where(me < last, 1, 0))

    @pl.when(me < last)
    def _():
        k_up(me, True).start()

    own_k.start()
    for lb in range(nb):
        for which in range(3):
            in_copy(lb, which).start()
    own_v.start()

    def prep(lb):
        for which in range(3):
            in_copy(lb, which).wait()

        def chunk(ci, _):
            span = pl.ds(ci * CH, CH)
            gc = g[lb, span]
            qt[lb, ci] = q[lb, span].T
            gt[lb, ci] = gc.T
            prod = gc.astype(jnp.float32) * o[lb, span].astype(jnp.float32)
            delta[lb, ci] = jnp.sum(prod.T, axis=0, keepdims=True)
            return 0

        lax.fori_loop(0, nch, chunk, 0)
        part_v[lb, TOPK] = jnp.zeros((BLK, hd), jnp.float32)
        part_k[lb, TOPK] = jnp.zeros((BLK, hd), jnp.float32)

    def pass_key(j):
        @pl.when(me >= j)
        def _():
            k_up(me - j, False).wait_recv()

            @pl.when(me < last)
            def _():
                k_up(me - j, False).start()

    done = 0
    for j in range(1, n):
        if done < nb:
            prep(done)
            done += 1
        pass_key(j)

    @pl.when(me < last)
    def _():
        v_up(me, True).start()

    for lb in range(done, nb):
        prep(lb)
    own_k.wait()

    def pass_value(j):
        @pl.when((me >= j) & (me < last))
        def _():
            v_up(me - j, False).wait_recv()
            v_up(me - j, False).start()

    def entry(lb, t):
        return lists[me * nb + lb, t]

    def phase_a(lb):
        kcat[0:BLK] = kfull[me * nb + lb]
        for t in range(1, TOPK):
            kcat[t * BLK : (t + 1) * BLK] = kfull[jnp.maximum(entry(lb, t), 0)]
        for t in range(TOPK):
            part_v[lb, t] = jnp.zeros((BLK, hd), jnp.float32)
        listed = [entry(lb, t) >= 0 for t in range(1, TOPK)]

        def chunk(ci, _):
            raw = jnp.dot(kcat[...], qt[lb, ci], preferred_element_type=jnp.float32)
            key = lax.broadcasted_iota(jnp.int32, (BLK, CH), 0)
            row = lax.broadcasted_iota(jnp.int32, (BLK, CH), 1) + ci * CH
            pieces = [jnp.where(key * heads <= row, raw[:BLK], -jnp.inf)]
            for t in range(1, TOPK):
                pieces.append(raw[t * BLK : (t + 1) * BLK])
            top = jnp.max(pieces[0], axis=0, keepdims=True)
            for t in range(1, TOPK):
                high = jnp.max(pieces[t], axis=0, keepdims=True)
                top = jnp.maximum(top, jnp.where(listed[t - 1], high, -jnp.inf))
            exps = []
            total = jnp.zeros((1, CH), jnp.float32)
            for t in range(TOPK):
                low = top if t == 0 else jnp.where(listed[t - 1], top, jnp.inf)
                e = jnp.exp2((pieces[t] - low) * (scaling * LOG2E))
                total = total + jnp.sum(e, axis=0, keepdims=True)
                exps.append(e)
            inv = 1.0 / total
            gc = g[lb, pl.ds(ci * CH, CH)]
            for t in range(TOPK):
                p = exps[t] * inv
                probs[lb, ci, t * BLK : (t + 1) * BLK] = p
                part_v[lb, t] += jnp.dot(
                    p.astype(jnp.bfloat16), gc, preferred_element_type=jnp.float32
                )
            return 0

        lax.fori_loop(0, nch, chunk, 0)

    def phase_b(lb):
        kcat[0:BLK] = kfull[me * nb + lb]
        vcat[0:BLK] = vfull[me * nb + lb]
        for t in range(1, TOPK):
            block = jnp.maximum(entry(lb, t), 0)
            kcat[t * BLK : (t + 1) * BLK] = kfull[block]
            vcat[t * BLK : (t + 1) * BLK] = vfull[block]
        kcat_t[...] = kcat[...].T
        for t in range(TOPK):
            part_k[lb, t] = jnp.zeros((BLK, hd), jnp.float32)

        def chunk(ci, _):
            span = pl.ds(ci * CH, CH)
            d_prob = jnp.dot(vcat[...], gt[lb, ci], preferred_element_type=jnp.float32)
            ds = (probs[lb, ci] * (d_prob - delta[lb, ci])).astype(jnp.bfloat16)
            qc = q[lb, span]
            for t in range(TOPK):
                part_k[lb, t] += jnp.dot(
                    ds[t * BLK : (t + 1) * BLK], qc, preferred_element_type=jnp.float32
                )
            dq_t = jnp.dot(kcat_t[...], ds, preferred_element_type=jnp.float32)
            o[lb, span] = (dq_t.T * scaling).astype(jnp.bfloat16)
            return 0

        lax.fori_loop(0, nch, chunk, 0)
        dq_copy(lb).start()

    def local_sum(part, block):
        total = None
        for lb in range(nb):
            slot = jnp.int32(TOPK)
            for t in range(TOPK):
                slot = jnp.where(entry(lb, t) == block, t, slot)
            term = part[lb, slot]
            total = term if total is None else total + term
        return total

    def chain(part, buf, copy, factor, owner):
        @pl.when(owner <= me)
        def _():
            @pl.when(me < last)
            def _():
                copy(owner).wait_recv()

                def add(i, _):
                    total = local_sum(part, owner * nb + i) + buf[owner, i].astype(jnp.float32)
                    buf[owner, i] = (total * jnp.where(owner == me, factor, 1.0)).astype(jnp.bfloat16)
                    return 0

                lax.fori_loop(0, nb, add, 0)

            @pl.when(me == last)
            def _():
                def add(i, _):
                    total = local_sum(part, owner * nb + i)
                    buf[owner, i] = (total * jnp.where(owner == me, factor, 1.0)).astype(jnp.bfloat16)
                    return 0

                lax.fori_loop(0, nb, add, 0)

            @pl.when(owner < me)
            def _():
                copy(owner).start()

    def dv_step(owner):
        chain(part_v, dvbuf, dv_down, 1.0, owner)

    def dk_step(owner):
        chain(part_k, dkbuf, dk_down, scaling, owner)

    def loop(low, high, step):
        def body(i, _):
            step(i)
            return 0

        if low < high:
            lax.fori_loop(low, high, body, 0)

    late = nb - 2
    loop(0, late + 1, phase_a)
    pass_value(1)
    loop(late + 1, nb, phase_a)
    loop(2, n, pass_value)

    @pl.when(me == last)
    def _():
        loop(0, n, dv_step)

        def arrive(j, _):
            v_up(me - j, False).wait_recv()
            return 0

        lax.fori_loop(1, n, arrive, 0)

    own_v.wait()

    half = nb // 2
    loop(0, half, phase_b)

    @pl.when(me < last)
    def _():
        dv_step(0)

    loop(half, nb, phase_b)

    @pl.when(me < last)
    def _():
        loop(1, n, dv_step)

    dv_out = pltpu.make_async_copy(dvbuf.at[me], dv_hbm, own_sem.at[1])
    dv_out.start()
    loop(0, n, dk_step)
    dk_out = pltpu.make_async_copy(dkbuf.at[me], dk_hbm, own_sem.at[0])
    dk_out.start()
    for lb in range(nb):
        dq_copy(lb).wait()

    def finish_up(j, _):
        @pl.when(j <= me)
        def _():
            @pl.when(me < last)
            def _():
                k_up(j, False).wait_send()
                v_up(j, False).wait_send()

        @pl.when(j < me)
        def _():
            dv_down(j).wait_send()
            dk_down(j).wait_send()

        return 0

    lax.fori_loop(0, n, finish_up, 0)
    dv_out.wait()
    dk_out.wait()


def shards(queries, keys, values, output, d_output, block_lists):
    tokens, heads, hd = queries.shape
    n = lax.axis_size("ctx")
    nb = tokens // BLK
    rows = BLK * heads
    nch = rows // CH
    flat = (nb, rows, hd)
    blocks = (nb, BLK, hd)
    bf16, f32 = jnp.bfloat16, jnp.float32
    dma = pltpu.SemaphoreType.DMA
    any_spec = pl.BlockSpec(memory_space=pl.ANY)
    pairs = nb * TOPK
    d_queries, d_keys, d_values = pl.pallas_call(
        functools.partial(kernel, n, nb, heads, hd),
        out_shape=(
            jax.ShapeDtypeStruct(flat, bf16),
            jax.ShapeDtypeStruct(blocks, bf16),
            jax.ShapeDtypeStruct(blocks, bf16),
        ),
        in_specs=[pl.BlockSpec(memory_space=pltpu.SMEM)] + [any_spec] * 5,
        out_specs=(any_spec,) * 3,
        scratch_shapes=[
            pltpu.VMEM(flat, bf16),
            pltpu.VMEM(flat, bf16),
            pltpu.VMEM(flat, bf16),
            pltpu.VMEM((nb, nch, hd, CH), bf16),
            pltpu.VMEM((nb, nch, hd, CH), bf16),
            pltpu.VMEM((nb, nch, 1, CH), f32),
            pltpu.VMEM((nb, nch, TOPK * BLK, CH), f32),
            pltpu.VMEM((n * nb, BLK, hd), bf16),
            pltpu.VMEM((n * nb, BLK, hd), bf16),
            pltpu.VMEM((TOPK * BLK, hd), bf16),
            pltpu.VMEM((hd, TOPK * BLK), bf16),
            pltpu.VMEM((TOPK * BLK, hd), bf16),
            pltpu.VMEM((nb, TOPK + 1, BLK, hd), f32),
            pltpu.VMEM((nb, TOPK + 1, BLK, hd), f32),
            pltpu.VMEM((n, nb, BLK, hd), bf16),
            pltpu.VMEM((n, nb, BLK, hd), bf16),
            dma((3, nb)),
            dma((nb,)),
            dma((2,)),
        ]
        + [dma((n,))] * 8,
        compiler_params=pltpu.CompilerParams(
            collective_id=0, has_side_effects=True, vmem_limit_bytes=63 * 1024 * 1024
        ),
        cost_estimate=pl.CostEstimate(
            flops=pairs * 5 * 2 * rows * BLK * hd,
            bytes_accessed=4 * tokens * heads * hd * 2 + 4 * tokens * hd * 2,
            transcendentals=pairs * rows * BLK,
        ),
    )(
        block_lists,
        queries.reshape(flat),
        keys.reshape(blocks),
        values.reshape(blocks),
        output.reshape(flat),
        d_output.reshape(flat),
    )
    return (
        d_queries.reshape(queries.shape),
        d_keys.reshape(keys.shape),
        d_values.reshape(values.shape),
    )


def solution(mesh):
    return jax.shard_map(
        shards,
        mesh=mesh,
        in_specs=(
            P(("dp", "ctx"), None, None),
            P(("dp", "ctx"), None),
            P(("dp", "ctx"), None),
            P(("dp", "ctx"), None, None),
            P(("dp", "ctx"), None, None),
            P("dp", None),
        ),
        out_specs=(P(("dp", "ctx"), None, None), P(("dp", "ctx"), None), P(("dp", "ctx"), None)),
        check_vma=False,
    )
```

time: 204 us -> 102 us (0.50)
  Pallas kernels: 0 us -> 95.3 us
  waiting for transfers between devices: 82.6 us -> 0 us
  matrix products: 42.1 us -> 0 us
  other arithmetic: 31.5 us -> 0 us
  between operations: 30 us -> 0.66 us
  local copies, waits for them, and re-layouts: 16.8 us -> 5.87 us
    pallas_call x0 -> x1, Pallas kernels: none -> 95.3 us  [shards(): pl.pallas_call(functools.partial(kernel, n, nb, heads, hd), out_shape=(ja...]
    reduce_scatter x1 -> x0, waiting for transfers between devices: 57.1 us -> none  [shards(): mine = lax.psum_scatter(grad_terms, 'ctx', scatter_dimension=0, tiled=True)]
    dot_general x60 -> x0, matrix products: 42.1 us -> none  [the longest x12 15 us: shards(): jnp.einsum('hqk,kd->qhd', d_scores, key_block, preferred_element_type=jnp...]
    all_gather x1 -> x0, waiting for transfers between devices: 25.5 us -> none  [shards(): everything = lax.all_gather(paired, 'ctx', axis=0, tiled=True)]
    dynamic_update_slice x12 -> x0, other arithmetic: 19.7 us -> none  [shards(): lax.dynamic_update_slice_in_dim(grad_terms, existing + jnp.concatenate([k...]
    unnamed x81 -> x8, local copies, waits for them, and re-layouts: 11.9 us -> 5.87 us
    reduce_sum x6 -> x0, other arithmetic: 5.99 us -> none  [the longest x4 3.91 us: shards(): total = total + exps[slot_index].sum(axis=2)]
    broadcast_in_dim x1 -> x0, local copies, waits for them, and re-layouts: 2.42 us -> none  [shards(): grad_terms = jnp.zeros((group_size * shard_rows, 2 * head_dim), jnp.float32)]
  transfers between devices with their start and end apart: 2 -> 0, of which waited for: 2 -> 0; matrix products, arithmetic and copies ran while one was open for 12% -> 0% of each run, Pallas kernels for 0% -> 0%
where the time goes in v1:
time: 102 us
  Pallas kernels  95.3 us (93%)
  local copies, waits for them, and re-layouts  5.87 us (6%)
    pallas_call x1, Pallas kernels, shards(): pl.pallas_call(functools.partial(kernel, n, nb, heads, hd), out_shape=(ja...  95.3 us
    unnamed x8, local copies, waits for them, and re-layouts  5.87 us

profile of v1, /device:TPU:0, one launch (start us, length us, event | category | flops | bytes accessed | tf_op | source)
XLA Modules:
  0.0 101.8 jit_solution(4937677182645982824)
XLA Ops:
  0.6 1.4 %copy.9.lists = s32[16,3]{1,0:T(8,128)} copy(s32[16,3]{0,1:T(4,128)} %param.11) | data formatting | bytes 384 | tf_op args[5]
  2.0 95.3 %shard_map.85 = (bf16[4,2048,128]{2,1,0:T(8,128)(2,1)}, bf16[4,256,128]{2,1,0:T(8,128)(2,1)}, bf16[4,256,128]{2,1,0:T(8,128)(2,1)}) custom-call(s32[16,3]{1,0:T(8,128)} %copy.9.lists, bf16[4,2048,128]{2,1,0:T(8,128)(2,1)} %bitcast.11, bf16[4,256,128]{2,1,0:T(8,128)(2,1)} %bitcast.14, bf16[4,256,128]{2,1,0:T(8,128)(2,1)} %bitcast.15, ...), custom_call_target="tpu_custom_call" | custom-call | flops 8053063680 | bytes 9437184 | tf_op jit(solution)/shard_map/pallas_call | solution.py:328
  97.3 0.0 copy-start.1
  97.3 0.0 copy-start
  97.3 3.1 %copy.13 = bf16[1024,8,128]{2,1,0:T(8,128)(2,1)} copy(bf16[1024,8,128]{2,1,0:T(8,128)(2,1)} %bitcast.8) | data formatting | bytes 4194304
  100.4 0.0 copy-done.1
  100.4 0.7 copy.14
  101.1 0.0 copy-done
  101.1 0.7 copy.15
Async XLA Ops:
  97.3 3.1 %copy-start.1 = (bf16[4,256,128]{2,1,0:T(8,128)(2,1)S(1)}, bf16[4,256,128]{2,1,0:T(8,128)(2,1)}, u32[]{:S(2)}) copy-start(bf16[4,256,128]{2,1,0:T(8,128)(2,1)} %get-tuple-element.7) | copy-start | bytes 786436
  97.3 3.8 %copy-start = (bf16[4,256,128]{2,1,0:T(8,128)(2,1)S(1)}, bf16[4,256,128]{2,1,0:T(8,128)(2,1)}, u32[]{:S(2)}) copy-start(bf16[4,256,128]{2,1,0:T(8,128)(2,1)} %get-tuple-element.8) | copy-start | bytes 786436

commit v2 on v1

v2 whole, which is shorter than its diff:
```python
import functools

import jax
import jax.numpy as jnp
from jax import lax
from jax.experimental import pallas as pl
from jax.experimental.pallas import tpu as pltpu
from jax.sharding import PartitionSpec as P

BLK = 256
TOPK = 3
CH = 256
MESH = pl.DeviceIdType.MESH
LOG2E = 1.4426950408889634


def kernel(
    n, nb, heads, hd,
    lists, q_hbm, k_hbm, v_hbm, o_hbm, g_hbm,
    dq_hbm, dk_hbm, dv_hbm,
    q, g, o, qt, gt, delta, top0, sum0, fac0, probs, kfull, vfull, kcat, kcat_t, vcat,
    part_v, part_k, dvbuf, dkbuf,
    in_sem, out_sem, own_sem,
    k_send, k_recv, v_send, v_recv, dv_send, dv_recv, dk_send, dk_recv,
):
    me = lax.axis_index("ctx")
    rows = BLK * heads
    nch = rows // CH
    scaling = hd ** (-0.5)
    last = n - 1

    def up(hbm, full, send, recv, owner, i, own):
        at = owner * nb + i
        return pltpu.make_async_remote_copy(
            src_ref=hbm.at[i] if own else full.at[at],
            dst_ref=full.at[at],
            send_sem=send.at[at],
            recv_sem=recv.at[at],
            device_id={"ctx": me + 1},
            device_id_type=MESH,
        )

    k_up = functools.partial(up, k_hbm, kfull, k_send, k_recv)
    v_up = functools.partial(up, v_hbm, vfull, v_send, v_recv)

    def down(buf, send, recv, at):
        return pltpu.make_async_remote_copy(
            src_ref=buf.at[at],
            dst_ref=buf.at[at],
            send_sem=send.at[at],
            recv_sem=recv.at[at],
            device_id={"ctx": me - 1},
            device_id_type=MESH,
        )

    dv_down = functools.partial(down, dvbuf, dv_send, dv_recv)
    dk_down = functools.partial(down, dkbuf, dk_send, dk_recv)

    def loop(low, high, step):
        def body(i, _):
            step(i)
            return 0

        if low < high:
            lax.fori_loop(low, high, body, 0)

    def in_copy(lb, which):
        src, dst = ((q_hbm, q), (g_hbm, g), (o_hbm, o))[which]
        return pltpu.make_async_copy(src.at[lb], dst.at[lb], in_sem.at[which, lb])

    def dq_copy(lb):
        return pltpu.make_async_copy(o.at[lb], dq_hbm.at[lb], out_sem.at[lb])

    own_k = pltpu.make_async_copy(k_hbm, kfull.at[pl.ds(me * nb, nb)], own_sem.at[0])
    own_v = pltpu.make_async_copy(v_hbm, vfull.at[pl.ds(me * nb, nb)], own_sem.at[1])

    barrier = pltpu.get_barrier_semaphore()

    @pl.when(me > 0)
    def _():
        pl.semaphore_signal(barrier, inc=1, device_id={"ctx": me - 1}, device_id_type=MESH)

    @pl.when(me < last)
    def _():
        pl.semaphore_signal(barrier, inc=1, device_id={"ctx": me + 1}, device_id_type=MESH)

    pl.semaphore_wait(barrier, jnp.where(me > 0, 1, 0) + jnp.where(me < last, 1, 0))

    @pl.when(me < last)
    def _():
        for i in range(nb):
            k_up(me, i, True).start()

    own_k.start()
    for lb in range(nb):
        for which in range(3):
            in_copy(lb, which).start()
    own_v.start()
    own_k.wait()

    def prep(lb):
        for which in range(3):
            in_copy(lb, which).wait()

        def chunk(ci, _):
            span = pl.ds(ci * CH, CH)
            gc = g[lb, span]
            qc_t = q[lb, span].T
            qt[lb, ci] = qc_t
            gt[lb, ci] = gc.T
            prod = gc.astype(jnp.float32) * o[lb, span].astype(jnp.float32)
            delta[lb, ci] = jnp.sum(prod.T, axis=0, keepdims=True)
            raw = jnp.dot(kfull[me * nb + lb], qc_t, preferred_element_type=jnp.float32)
            key = lax.broadcasted_iota(jnp.int32, (BLK, CH), 0)
            row = lax.broadcasted_iota(jnp.int32, (BLK, CH), 1) + ci * CH
            raw = jnp.where(key * heads <= row, raw, -jnp.inf)
            top = jnp.max(raw, axis=0, keepdims=True)
            e = jnp.exp2((raw - top) * (scaling * LOG2E))
            probs[lb, ci, 0:BLK] = e
            top0[lb, ci] = top
            sum0[lb, ci] = jnp.sum(e, axis=0, keepdims=True)
            return 0

        lax.fori_loop(0, nch, chunk, 0, unroll=2)
        part_v[lb, TOPK] = jnp.zeros((BLK, hd), jnp.float32)
        part_k[lb, TOPK] = jnp.zeros((BLK, hd), jnp.float32)

    def pass_key(j):
        @pl.when(me >= j)
        def _():
            def one(i):
                k_up(me - j, i, False).wait_recv()

                @pl.when(me < last)
                def _():
                    k_up(me - j, i, False).start()

            loop(0, nb, one)

    loop(0, 2, prep)
    pass_key(1)
    loop(2, nb, prep)
    loop(2, n, pass_key)

    @pl.when(me < last)
    def _():
        for i in range(nb):
            v_up(me, i, True).start()

    def pass_value(j):
        @pl.when((me >= j) & (me < last))
        def _():
            def one(i):
                v_up(me - j, i, False).wait_recv()
                v_up(me - j, i, False).start()

            loop(0, nb, one)

    def entry(lb, t):
        return lists[me * nb + lb, t]

    def phase_a(lb):
        for t in range(1, TOPK):
            kcat[t * BLK : (t + 1) * BLK] = kfull[jnp.maximum(entry(lb, t), 0)]
            part_v[lb, t] = jnp.zeros((BLK, hd), jnp.float32)
        listed = [entry(lb, t) >= 0 for t in range(1, TOPK)]

        def chunk(ci, _):
            raw = jnp.dot(kcat[BLK:], qt[lb, ci], preferred_element_type=jnp.float32)
            first = top0[lb, ci]
            top = first
            for t in range(TOPK - 1):
                high = jnp.max(raw[t * BLK : (t + 1) * BLK], axis=0, keepdims=True)
                top = jnp.maximum(top, jnp.where(listed[t], high, -jnp.inf))
            shrink = jnp.exp2((first - top) * (scaling * LOG2E))
            total = sum0[lb, ci] * shrink
            exps = []
            for t in range(TOPK - 1):
                low = jnp.where(listed[t], top, jnp.inf)
                e = jnp.exp2((raw[t * BLK : (t + 1) * BLK] - low) * (scaling * LOG2E))
                total = total + jnp.sum(e, axis=0, keepdims=True)
                exps.append(e)
            inv = 1.0 / total
            fac0[lb, ci] = shrink * inv
            gc = g[lb, pl.ds(ci * CH, CH)]
            for t in range(1, TOPK):
                p = exps[t - 1] * inv
                probs[lb, ci, t * BLK : (t + 1) * BLK] = p
                part_v[lb, t] += jnp.dot(
                    p.astype(jnp.bfloat16), gc, preferred_element_type=jnp.float32
                )
            return 0

        lax.fori_loop(0, nch, chunk, 0, unroll=2)

    def phase_b(lb):
        kcat[0:BLK] = kfull[me * nb + lb]
        vcat[0:BLK] = vfull[me * nb + lb]
        for t in range(1, TOPK):
            block = jnp.maximum(entry(lb, t), 0)
            kcat[t * BLK : (t + 1) * BLK] = kfull[block]
            vcat[t * BLK : (t + 1) * BLK] = vfull[block]
        kcat_t[...] = kcat[...].T
        for t in range(TOPK):
            part_k[lb, t] = jnp.zeros((BLK, hd), jnp.float32)
        part_v[lb, 0] = jnp.zeros((BLK, hd), jnp.float32)

        def chunk(ci, _):
            span = pl.ds(ci * CH, CH)
            d_prob = jnp.dot(vcat[...], gt[lb, ci], preferred_element_type=jnp.float32)
            qc = q[lb, span]
            dq_t = jnp.zeros((hd, CH), jnp.float32)
            for t in range(TOPK):
                part = slice(t * BLK, (t + 1) * BLK)
                p = probs[lb, ci, part]
                if t == 0:
                    p = p * fac0[lb, ci]
                    part_v[lb, 0] += jnp.dot(
                        p.astype(jnp.bfloat16), g[lb, span], preferred_element_type=jnp.float32
                    )
                ds = (p * (d_prob[part] - delta[lb, ci])).astype(jnp.bfloat16)
                part_k[lb, t] += jnp.dot(ds, qc, preferred_element_type=jnp.float32)
                dq_t = dq_t + jnp.dot(kcat_t[:, part], ds, preferred_element_type=jnp.float32)
            o[lb, span] = (dq_t.T * scaling).astype(jnp.bfloat16)
            return 0

        lax.fori_loop(0, nch, chunk, 0, unroll=2)
        dq_copy(lb).start()

    def local_sum(part, block):
        total = None
        for lb in range(nb):
            slot = jnp.int32(TOPK)
            for t in range(TOPK):
                slot = jnp.where(entry(lb, t) == block, t, slot)
            term = part[lb, slot]
            total = term if total is None else total + term
        return total

    def chain(part, buf, copy, factor, owner):
        def one(i):
            at = owner * nb + i

            def put(total):
                buf[at] = (total * jnp.where(owner == me, factor, 1.0)).astype(jnp.bfloat16)

            @pl.when(me < last)
            def _():
                copy(at).wait_recv()
                put(local_sum(part, at) + buf[at].astype(jnp.float32))

            @pl.when(me == last)
            def _():
                put(local_sum(part, at))

            @pl.when(owner < me)
            def _():
                copy(at).start()

        @pl.when(owner <= me)
        def _():
            loop(0, nb, one)

    def dv_step(owner):
        chain(part_v, dvbuf, dv_down, 1.0, owner)

    def dk_step(owner):
        chain(part_k, dkbuf, dk_down, scaling, owner)

    late = nb - 2
    loop(0, late, phase_a)
    pass_value(1)
    loop(late, nb - 1, phase_a)
    if n > 2:
        pass_value(2)
    phase_a(nb - 1)
    loop(3, n, pass_value)

    @pl.when(me == last)
    def _():
        loop(0, n - 1, dv_step)

        def arrive(j):
            loop(0, nb, lambda i: v_up(me - j, i, False).wait_recv())

        loop(1, n, arrive)

    own_v.wait()

    half = nb // 2
    loop(0, half, phase_b)

    @pl.when((me > 0) & (me < last))
    def _():
        dv_step(0)

    loop(half, nb, phase_b)

    @pl.when(me == 0)
    def _():
        dv_step(0)

    @pl.when((me > 0) & (me < last))
    def _():
        loop(1, n, dv_step)

    @pl.when(me == last)
    def _():
        loop(0, n, dk_step)
        dv_step(last)

    dv_out = pltpu.make_async_copy(dvbuf.at[pl.ds(me * nb, nb)], dv_hbm, own_sem.at[1])
    dv_out.start()

    @pl.when(me < last)
    def _():
        loop(0, n, dk_step)

    dk_out = pltpu.make_async_copy(dkbuf.at[pl.ds(me * nb, nb)], dk_hbm, own_sem.at[0])
    dk_out.start()
    for lb in range(nb):
        dq_copy(lb).wait()

    def finish_up(j):
        def one(i):
            @pl.when((j <= me) & (me < last))
            def _():
                k_up(j, i, False).wait_send()
                v_up(j, i, False).wait_send()

            @pl.when(j < me)
            def _():
                dv_down(j * nb + i).wait_send()
                dk_down(j * nb + i).wait_send()

        loop(0, nb, one)

    loop(0, n, finish_up)
    dv_out.wait()
    dk_out.wait()


def shards(queries, keys, values, output, d_output, block_lists):
    tokens, heads, hd = queries.shape
    n = lax.axis_size("ctx")
    nb = tokens // BLK
    rows = BLK * heads
    nch = rows // CH
    flat = (nb, rows, hd)
    blocks = (nb, BLK, hd)
    bf16, f32 = jnp.bfloat16, jnp.float32
    dma = pltpu.SemaphoreType.DMA
    any_spec = pl.BlockSpec(memory_space=pl.ANY)
    pairs = nb * TOPK
    d_queries, d_keys, d_values = pl.pallas_call(
        functools.partial(kernel, n, nb, heads, hd),
        out_shape=(
            jax.ShapeDtypeStruct(flat, bf16),
            jax.ShapeDtypeStruct(blocks, bf16),
            jax.ShapeDtypeStruct(blocks, bf16),
        ),
        in_specs=[pl.BlockSpec(memory_space=pltpu.SMEM)] + [any_spec] * 5,
        out_specs=(any_spec,) * 3,
        scratch_shapes=[
            pltpu.VMEM(flat, bf16),
            pltpu.VMEM(flat, bf16),
            pltpu.VMEM(flat, bf16),
            pltpu.VMEM((nb, nch, hd, CH), bf16),
            pltpu.VMEM((nb, nch, hd, CH), bf16),
            pltpu.VMEM((nb, nch, 1, CH), f32),
            pltpu.VMEM((nb, nch, 1, CH), f32),
            pltpu.VMEM((nb, nch, 1, CH), f32),
            pltpu.VMEM((nb, nch, 1, CH), f32),
            pltpu.VMEM((nb, nch, TOPK * BLK, CH), f32),
            pltpu.VMEM((n * nb, BLK, hd), bf16),
            pltpu.VMEM((n * nb, BLK, hd), bf16),
            pltpu.VMEM((TOPK * BLK, hd), bf16),
            pltpu.VMEM((hd, TOPK * BLK), bf16),
            pltpu.VMEM((TOPK * BLK, hd), bf16),
            pltpu.VMEM((nb, TOPK + 1, BLK, hd), f32),
            pltpu.VMEM((nb, TOPK + 1, BLK, hd), f32),
            pltpu.VMEM((n * nb, BLK, hd), bf16),
            pltpu.VMEM((n * nb, BLK, hd), bf16),
            dma((3, nb)),
            dma((nb,)),
            dma((2,)),
        ]
        + [dma((n * nb,))] * 8,
        compiler_params=pltpu.CompilerParams(
            collective_id=0, has_side_effects=True, vmem_limit_bytes=63 * 1024 * 1024
        ),
        cost_estimate=pl.CostEstimate(
            flops=pairs * 5 * 2 * rows * BLK * hd,
            bytes_accessed=4 * tokens * heads * hd * 2 + 4 * tokens * hd * 2,
            transcendentals=pairs * rows * BLK,
        ),
    )(
        block_lists,
        queries.reshape(flat),
        keys.reshape(blocks),
        values.reshape(blocks),
        output.reshape(flat),
        d_output.reshape(flat),
    )
    return (
        d_queries.reshape(queries.shape),
        d_keys.reshape(keys.shape),
        d_values.reshape(values.shape),
    )


def solution(mesh):
    return jax.shard_map(
        shards,
        mesh=mesh,
        in_specs=(
            P(("dp", "ctx"), None, None),
            P(("dp", "ctx"), None),
            P(("dp", "ctx"), None),
            P(("dp", "ctx"), None, None),
            P(("dp", "ctx"), None, None),
            P("dp", None),
        ),
        out_specs=(P(("dp", "ctx"), None, None), P(("dp", "ctx"), None), P(("dp", "ctx"), None)),
        check_vma=False,
    )
```

time: 102 us -> 80.2 us (0.79)
  Pallas kernels: 95.3 us -> 73.4 us
    pallas_call x1, Pallas kernels: 95.3 us -> 73.4 us  [shards(): pl.pallas_call(functools.partial(kernel, n, nb, heads, hd), out_shape=(ja...]
where the time goes in v2:
time: 80.2 us; the launch traced here: 79.9 us
  Pallas kernels  73.4 us (92%)
  local copies, waits for them, and re-layouts  5.87 us (7%)
    pallas_call x1, Pallas kernels, shards(): pl.pallas_call(functools.partial(kernel, n, nb, heads, hd), out_shape=(ja...  73.4 us
    unnamed x8, local copies, waits for them, and re-layouts  5.87 us

profile of v2, /device:TPU:0, one launch (start us, length us, event | category | flops | bytes accessed | tf_op | source)
XLA Modules:
  0.0 79.9 jit_solution(13408499549680639535)
XLA Ops:
  0.6 1.4 %copy.9.lists = s32[16,3]{1,0:T(8,128)} copy(s32[16,3]{0,1:T(4,128)} %param.11) | data formatting | bytes 384 | tf_op args[5]
  2.0 73.4 %shard_map.85 = (bf16[4,2048,128]{2,1,0:T(8,128)(2,1)}, bf16[4,256,128]{2,1,0:T(8,128)(2,1)}, bf16[4,256,128]{2,1,0:T(8,128)(2,1)}) custom-call(s32[16,3]{1,0:T(8,128)} %copy.9.lists, bf16[4,2048,128]{2,1,0:T(8,128)(2,1)} %bitcast.11, bf16[4,256,128]{2,1,0:T(8,128)(2,1)} %bitcast.14, bf16[4,256,128]{2,1,0:T(8,128)(2,1)} %bitcast.15, ...), custom_call_target="tpu_custom_call" | custom-call | flops 8053063680 | bytes 9437184 | tf_op jit(solution)/shard_map/pallas_call | solution.py:355
  75.4 0.0 copy-start.1
  75.4 0.0 copy-start
  75.4 3.1 %copy.13 = bf16[1024,8,128]{2,1,0:T(8,128)(2,1)} copy(bf16[1024,8,128]{2,1,0:T(8,128)(2,1)} %bitcast.8) | data formatting | bytes 4194304
  78.5 0.0 copy-done.1
  78.5 0.7 copy.14
  79.2 0.0 copy-done
  79.2 0.7 copy.15
Async XLA Ops:
  75.4 3.1 %copy-start.1 = (bf16[4,256,128]{2,1,0:T(8,128)(2,1)S(1)}, bf16[4,256,128]{2,1,0:T(8,128)(2,1)}, u32[]{:S(2)}) copy-start(bf16[4,256,128]{2,1,0:T(8,128)(2,1)} %get-tuple-element.7) | copy-start | bytes 786436
  75.4 3.8 %copy-start = (bf16[4,256,128]{2,1,0:T(8,128)(2,1)S(1)}, bf16[4,256,128]{2,1,0:T(8,128)(2,1)}, u32[]{:S(2)}) copy-start(bf16[4,256,128]{2,1,0:T(8,128)(2,1)} %get-tuple-element.8) | copy-start | bytes 786436

commit v3 on v2

--- a/solution.py
+++ b/solution.py
@@ -19,15 +19,17 @@
     lists, q_hbm, k_hbm, v_hbm, o_hbm, g_hbm,
     dq_hbm, dk_hbm, dv_hbm,
     q, g, o, qt, gt, delta, top0, sum0, fac0, probs, kfull, vfull, kcat, kcat_t, vcat,
-    part_v, part_k, dvbuf, dkbuf,
+    part_v, part_k, dvbuf, dkbuf, dvslot, dkslot, rank,
     in_sem, out_sem, own_sem,
     k_send, k_recv, v_send, v_recv, dv_send, dv_recv, dk_send, dk_recv,
+    dvs_send, dvs_recv, dks_send, dks_recv,
 ):
     me = lax.axis_index("ctx")
     rows = BLK * heads
     nch = rows // CH
     scaling = hd ** (-0.5)
     last = n - 1
+    slots = min((TOPK - 1) * nb, last * nb)
 
     def up(hbm, full, send, recv, owner, i, own):
         at = owner * nb + i
@@ -55,6 +57,8 @@
 
     dv_down = functools.partial(down, dvbuf, dv_send, dv_recv)
     dk_down = functools.partial(down, dkbuf, dk_send, dk_recv)
+    dv_slot = functools.partial(down, dvslot, dvs_send, dvs_recv)
+    dk_slot = functools.partial(down, dkslot, dks_send, dks_recv)
 
     def loop(low, high, step):
         def body(i, _):
@@ -97,6 +101,16 @@
             in_copy(lb, which).start()
     own_v.start()
     own_k.wait()
+
+    def count(block, seen):
+        hit = jnp.bool_(False)
+        for lb in range(nb):
+            for t in range(1, TOPK):
+                hit = hit | (lists[t, last * nb + lb] == block)
+        rank[block] = jnp.where(hit, seen, -1)
+        return seen + jnp.where(hit, 1, 0)
+
+    lax.fori_loop(0, last * nb, count, jnp.int32(0))
 
     def prep(lb):
         for which in range(3):
@@ -157,7 +171,7 @@
             loop(0, nb, one)
 
     def entry(lb, t):
-        return lists[me * nb + lb, t]
+        return lists[t, me * nb + lb]
 
     def phase_a(lb):
         for t in range(1, TOPK):
@@ -194,13 +208,10 @@
         lax.fori_loop(0, nch, chunk, 0, unroll=2)
 
     def phase_b(lb):
-        kcat[0:BLK] = kfull[me * nb + lb]
         vcat[0:BLK] = vfull[me * nb + lb]
         for t in range(1, TOPK):
             block = jnp.maximum(entry(lb, t), 0)
-            kcat[t * BLK : (t + 1) * BLK] = kfull[block]
             vcat[t * BLK : (t + 1) * BLK] = vfull[block]
-        kcat_t[...] = kcat[...].T
         for t in range(TOPK):
             part_k[lb, t] = jnp.zeros((BLK, hd), jnp.float32)
         part_v[lb, 0] = jnp.zeros((BLK, hd), jnp.float32)
@@ -209,7 +220,6 @@
             span = pl.ds(ci * CH, CH)
             d_prob = jnp.dot(vcat[...], gt[lb, ci], preferred_element_type=jnp.float32)
             qc = q[lb, span]
-            dq_t = jnp.zeros((hd, CH), jnp.float32)
             for t in range(TOPK):
                 part = slice(t * BLK, (t + 1) * BLK)
                 p = probs[lb, ci, part]
@@ -220,8 +230,21 @@
                     )
                 ds = (p * (d_prob[part] - delta[lb, ci])).astype(jnp.bfloat16)
                 part_k[lb, t] += jnp.dot(ds, qc, preferred_element_type=jnp.float32)
-                dq_t = dq_t + jnp.dot(kcat_t[:, part], ds, preferred_element_type=jnp.float32)
-            o[lb, span] = (dq_t.T * scaling).astype(jnp.bfloat16)
+                probs[lb, ci, part] = ds.astype(jnp.float32)
+            return 0
+
+        lax.fori_loop(0, nch, chunk, 0, unroll=2)
+
+    def dq_pass(lb):
+        kcat[0:BLK] = kfull[me * nb + lb]
+        for t in range(1, TOPK):
+            kcat[t * BLK : (t + 1) * BLK] = kfull[jnp.maximum(entry(lb, t), 0)]
+        kcat_t[...] = kcat[...].T
+
+        def chunk(ci, _):
+            ds = probs[lb, ci].astype(jnp.bfloat16)
+            dq_t = jnp.dot(kcat_t[...], ds, preferred_element_type=jnp.float32)
+            o[lb, pl.ds(ci * CH, CH)] = (dq_t.T * scaling).astype(jnp.bfloat16)
             return 0
 
         lax.fori_loop(0, nch, chunk, 0, unroll=2)
@@ -237,23 +260,36 @@
             total = term if total is None else total + term
         return total
 
-    def chain(part, buf, copy, factor, owner):
+    def chain(part, buf, copy, slot, slot_copy, factor, owner):
         def one(i):
             at = owner * nb + i
 
             def put(total):
                 buf[at] = (total * jnp.where(owner == me, factor, 1.0)).astype(jnp.bfloat16)
 
-            @pl.when(me < last)
+            @pl.when(me < last - 1)
             def _():
                 copy(at).wait_recv()
                 put(local_sum(part, at) + buf[at].astype(jnp.float32))
 
+            @pl.when(me == last - 1)
+            def _():
+                @pl.when(at < slots)
+                def _():
+                    slot_copy(at).wait_recv()
+
+                mine = rank[at]
+
+                def pick(s, total):
+                    return total + jnp.where(mine == s, slot[s].astype(jnp.float32), 0.0)
+
+                put(lax.fori_loop(0, jnp.minimum(at + 1, slots), pick, local_sum(part, at)))
+
             @pl.when(me == last)
             def _():
                 put(local_sum(part, at))
 
-            @pl.when(owner < me)
+            @pl.when((owner < me) & (me < last))
             def _():
                 copy(at).start()
 
@@ -261,11 +297,21 @@
         def _():
             loop(0, nb, one)
 
+    def send_slots(part, slot, slot_copy):
+        def one(s):
+            block = lax.fori_loop(
+                0, last * nb, lambda b, got: jnp.where(rank[b] == s, b, got), jnp.int32(-2)
+            )
+            slot[s] = local_sum(part, block).astype(jnp.bfloat16)
+            slot_copy(s).start()
+
+        loop(0, slots, one)
+
     def dv_step(owner):
-        chain(part_v, dvbuf, dv_down, 1.0, owner)
+        chain(part_v, dvbuf, dv_down, dvslot, dv_slot, 1.0, owner)
 
     def dk_step(owner):
-        chain(part_k, dkbuf, dk_down, scaling, owner)
+        chain(part_k, dkbuf, dk_down, dkslot, dk_slot, scaling, owner)
 
     late = nb - 2
     loop(0, late, phase_a)
@@ -278,7 +324,7 @@
 
     @pl.when(me == last)
     def _():
-        loop(0, n - 1, dv_step)
+        send_slots(part_v, dvslot, dv_slot)
 
         def arrive(j):
             loop(0, nb, lambda i: v_up(me - j, i, False).wait_recv())
@@ -300,14 +346,20 @@
     def _():
         dv_step(0)
 
+    @pl.when(me < last)
+    def _():
+        loop(0, nb, dq_pass)
+
     @pl.when((me > 0) & (me < last))
     def _():
         loop(1, n, dv_step)
 
     @pl.when(me == last)
     def _():
-        loop(0, n, dk_step)
+        send_slots(part_k, dkslot, dk_slot)
+        dk_step(last)
         dv_step(last)
+        loop(0, nb, dq_pass)
 
     dv_out = pltpu.make_async_copy(dvbuf.at[pl.ds(me * nb, nb)], dv_hbm, own_sem.at[1])
     dv_out.start()
@@ -328,10 +380,15 @@
                 k_up(j, i, False).wait_send()
                 v_up(j, i, False).wait_send()
 
-            @pl.when(j < me)
+            @pl.when((j < me) & (me < last))
             def _():
                 dv_down(j * nb + i).wait_send()
                 dk_down(j * nb + i).wait_send()
+
+            @pl.when((me == last) & (j * nb + i < slots))
+            def _():
+                dv_slot(j * nb + i).wait_send()
+                dk_slot(j * nb + i).wait_send()
 
         loop(0, nb, one)
 
@@ -352,6 +409,7 @@
     dma = pltpu.SemaphoreType.DMA
     any_spec = pl.BlockSpec(memory_space=pl.ANY)
     pairs = nb * TOPK
+    slots = min((TOPK - 1) * nb, (n - 1) * nb)
     d_queries, d_keys, d_values = pl.pallas_call(
         functools.partial(kernel, n, nb, heads, hd),
         out_shape=(
@@ -381,11 +439,15 @@
             pltpu.VMEM((nb, TOPK + 1, BLK, hd), f32),
             pltpu.VMEM((n * nb, BLK, hd), bf16),
             pltpu.VMEM((n * nb, BLK, hd), bf16),
+            pltpu.VMEM((slots, BLK, hd), bf16),
+            pltpu.VMEM((slots, BLK, hd), bf16),
+            pltpu.SMEM(((n - 1) * nb,), jnp.int32),
             dma((3, nb)),
             dma((nb,)),
             dma((2,)),
         ]
-        + [dma((n * nb,))] * 8,
+        + [dma((n * nb,))] * 8
+        + [dma((slots,))] * 4,
         compiler_params=pltpu.CompilerParams(
             collective_id=0, has_side_effects=True, vmem_limit_bytes=63 * 1024 * 1024
         ),
@@ -395,7 +457,7 @@
             transcendentals=pairs * rows * BLK,
         ),
     )(
-        block_lists,
+        block_lists.T,
         queries.reshape(flat),
         keys.reshape(blocks),
         values.reshape(blocks),

time: 80.2 us -> 81.2 us (1.012)
  Pallas kernels: 73.4 us -> 75.8 us
  local copies, waits for them, and re-layouts: 5.87 us -> 4.51 us
    pallas_call x1, Pallas kernels: 73.4 us -> 75.8 us  [shards(): pl.pallas_call(functools.partial(kernel, n, nb, heads, hd), out_shape=(ja...]
    unnamed x8 -> x7, local copies, waits for them, and re-layouts: 5.87 us -> 4.51 us
where the time goes in v3:
time: 81.2 us; the launch traced here: 81 us
  Pallas kernels  75.8 us (93%)
  local copies, waits for them, and re-layouts  4.51 us (6%)
    pallas_call x1, Pallas kernels, shards(): pl.pallas_call(functools.partial(kernel, n, nb, heads, hd), out_shape=(ja...  75.8 us
    unnamed x7, local copies, waits for them, and re-layouts  4.51 us

profile of v3, /device:TPU:0, one launch (start us, length us, event | category | flops | bytes accessed | tf_op | source)
XLA Modules:
  0.0 81.0 jit_solution(18265677488593563679)
XLA Ops:
  0.6 75.8 %shard_map.85 = (bf16[4,2048,128]{2,1,0:T(8,128)(2,1)}, bf16[4,256,128]{2,1,0:T(8,128)(2,1)}, bf16[4,256,128]{2,1,0:T(8,128)(2,1)}) custom-call(s32[3,16]{1,0:T(4,128)} %bitcast.17, bf16[4,2048,128]{2,1,0:T(8,128)(2,1)} %bitcast.12, bf16[4,256,128]{2,1,0:T(8,128)(2,1)} %bitcast.15, bf16[4,256,128]{2,1,0:T(8,128)(2,1)} %bitcast.16, ...), custom_call_target="tpu_custom_call" | custom-call | flops 8053063680 | bytes 9437184 | tf_op jit(solution)/shard_map/pallas_call | solution.py:413
  76.4 0.0 copy-start.1
  76.5 0.0 copy-start
  76.5 3.1 %copy.12 = bf16[1024,8,128]{2,1,0:T(8,128)(2,1)} copy(bf16[1024,8,128]{2,1,0:T(8,128)(2,1)} %bitcast.9) | data formatting | bytes 4194304
  79.6 0.0 copy-done.1
  79.6 0.7 copy.13
  80.3 0.0 copy-done
  80.3 0.7 copy.14
Async XLA Ops:
  76.4 3.1 %copy-start.1 = (bf16[4,256,128]{2,1,0:T(8,128)(2,1)S(1)}, bf16[4,256,128]{2,1,0:T(8,128)(2,1)}, u32[]{:S(2)}) copy-start(bf16[4,256,128]{2,1,0:T(8,128)(2,1)} %get-tuple-element.7) | copy-start | bytes 786436
  76.5 3.8 %copy-start = (bf16[4,256,128]{2,1,0:T(8,128)(2,1)S(1)}, bf16[4,256,128]{2,1,0:T(8,128)(2,1)}, u32[]{:S(2)}) copy-start(bf16[4,256,128]{2,1,0:T(8,128)(2,1)} %get-tuple-element.8) | copy-start | bytes 786436

commit v4 on v3

--- a/solution.py
+++ b/solution.py
@@ -336,23 +336,25 @@
     half = nb // 2
     loop(0, half, phase_b)
 
-    @pl.when((me > 0) & (me < last))
+    @pl.when((me > 0) & (me == last - 1))
     def _():
         dv_step(0)
 
     loop(half, nb, phase_b)
 
-    @pl.when(me == 0)
-    def _():
-        dv_step(0)
+    @pl.when((me > 0) & (me == last - 1))
+    def _():
+        loop(1, n, dv_step)
 
     @pl.when(me < last)
     def _():
         loop(0, nb, dq_pass)
 
-    @pl.when((me > 0) & (me < last))
-    def _():
-        loop(1, n, dv_step)
+    @pl.when((me == 0) | (me < last - 1))
+    def _():
+        @pl.when(me < last)
+        def _():
+            loop(0, n, dv_step)
 
     @pl.when(me == last)
     def _():

time: 81.2 us -> 79.1 us (0.974)
  Pallas kernels: 75.8 us -> 73.8 us
    pallas_call x1, Pallas kernels: 75.8 us -> 73.8 us  [shards(): pl.pallas_call(functools.partial(kernel, n, nb, heads, hd), out_shape=(ja...]
where the time goes in v4:
time: 79.1 us; the launch traced here: 78.9 us
  Pallas kernels  73.8 us (93%)
  local copies, waits for them, and re-layouts  4.51 us (6%)
    pallas_call x1, Pallas kernels, shards(): pl.pallas_call(functools.partial(kernel, n, nb, heads, hd), out_shape=(ja...  73.8 us
    unnamed x7, local copies, waits for them, and re-layouts  4.51 us

profile of v4, /device:TPU:0, one launch (start us, length us, event | category | flops | bytes accessed | tf_op | source)
XLA Modules:
  0.0 78.9 jit_solution(17489687150537495261)
XLA Ops:
  0.6 73.8 %shard_map.85 = (bf16[4,2048,128]{2,1,0:T(8,128)(2,1)}, bf16[4,256,128]{2,1,0:T(8,128)(2,1)}, bf16[4,256,128]{2,1,0:T(8,128)(2,1)}) custom-call(s32[3,16]{1,0:T(4,128)} %bitcast.17, bf16[4,2048,128]{2,1,0:T(8,128)(2,1)} %bitcast.12, bf16[4,256,128]{2,1,0:T(8,128)(2,1)} %bitcast.15, bf16[4,256,128]{2,1,0:T(8,128)(2,1)} %bitcast.16, ...), custom_call_target="tpu_custom_call" | custom-call | flops 8053063680 | bytes 9437184 | tf_op jit(solution)/shard_map/pallas_call | solution.py:415
  74.4 0.0 copy-start.1
  74.4 0.0 copy-start
  74.4 3.1 %copy.12 = bf16[1024,8,128]{2,1,0:T(8,128)(2,1)} copy(bf16[1024,8,128]{2,1,0:T(8,128)(2,1)} %bitcast.9) | data formatting | bytes 4194304
  77.5 0.0 copy-done.1
  77.5 0.7 copy.13
  78.2 0.0 copy-done
  78.2 0.7 copy.14
Async XLA Ops:
  74.4 3.1 %copy-start.1 = (bf16[4,256,128]{2,1,0:T(8,128)(2,1)S(1)}, bf16[4,256,128]{2,1,0:T(8,128)(2,1)}, u32[]{:S(2)}) copy-start(bf16[4,256,128]{2,1,0:T(8,128)(2,1)} %get-tuple-element.7) | copy-start | bytes 786436
  74.4 3.8 %copy-start = (bf16[4,256,128]{2,1,0:T(8,128)(2,1)S(1)}, bf16[4,256,128]{2,1,0:T(8,128)(2,1)}, u32[]{:S(2)}) copy-start(bf16[4,256,128]{2,1,0:T(8,128)(2,1)} %get-tuple-element.8) | copy-start | bytes 786436
